TPU v7x, 32 devices: a whole 2x2x4 slice. The times are simulated.
32 devices in a mesh: user: 4 (over y, core), party: 8 (over z, x).
Axes of the slice: x: 2, y: 2, z: 4, core: 2. Of those that a mesh axis runs over, the one named last changes fastest.
Arguments:
- ratings: bfloat16 [512, 4096], P('party', 'user'), may hold values from -6 to 6
- rating_mask: int32 [512, 4096], P('party', 'user'), may hold values 0 or 1
- user_factors: bfloat16 [4096, 256], P('user'), may hold values from -0.375 to 0.375
- item_factors: bfloat16 [512, 256], replicated, may hold values from -6 to 6
- item_index: int32 [512], replicated, may hold values from 0 to 511, each once
- features: bfloat16 [512, 524288], P(None, ('user', 'party')), may hold values from -6 to 6
- ridge_weights: bfloat16 [524288, 256], P(('user', 'party')), may hold values from -10 to 10
Outputs:
- new_factors: float32 [512, 256], P('party')
- fitted_weights: float32 [524288, 256], P(('user', 'party'))
Inputs may be any that keep to these rules, and one draw needn't show every extreme that they name: `item_index`: each window item stands at exactly one tile position.
All inputs are finite; a program needn't handle non-finite values. No bound on the sum of `rating_mask` on one device may be relied on, other than what follows from the above.
Results may differ from a plain program's by a relative error of at most 0.00032.
Values may be sent and summed in bfloat16 or wider, within the bound.
A program may use at most 128 MiB of HBM per device.

v0:
```python
import jax
import jax.numpy as jnp
from jax import lax
from jax.sharding import PartitionSpec as P

ITERS = 2


learn_rate = 0.05
factor_decay = 1.0
ridge_decay = 0.05
ridge_step = 0.05


def local(ratings, rating_mask, user_factors, item_factors, item_index, features, ridge_weights):
    local_items = ratings.shape[0]
    party_pos = lax.axis_index("party")
    local_index = lax.dynamic_slice_in_dim(item_index, party_pos * local_items, local_items)
    tile_rows = jnp.take(item_factors, local_index, axis=0)
    scores = lax.dot_general(
        tile_rows, user_factors, (((1,), (1,)), ((), ())), preferred_element_type=jnp.float32
    )
    misfit = (rating_mask.astype(jnp.float32) * (scores - ratings.astype(jnp.float32))).astype(
        jnp.bfloat16
    )
    partial_grad = jnp.dot(misfit, user_factors, preferred_element_type=jnp.float32)
    grad_share = lax.psum_scatter(partial_grad, "user", scatter_dimension=0, tiled=True)
    row_count = grad_share.shape[0]
    own_rows = lax.dynamic_slice_in_dim(
        tile_rows, lax.axis_index("user") * row_count, row_count
    ).astype(jnp.float32)
    own_new = own_rows - learn_rate * (grad_share + factor_decay * own_rows)
    new_factors = lax.all_gather(own_new, "user", axis=0, tiled=True)
    all_factors = lax.all_gather(new_factors, "party", axis=0, tiled=True)
    targets = jnp.zeros(all_factors.shape, jnp.float32).at[item_index].set(all_factors)
    devices_all = lax.axis_size(("user", "party"))
    total_features = features.shape[1] * devices_all
    feature_scale = 1.0 / float(total_features) ** 0.5
    weights = ridge_weights.astype(jnp.float32)
    for iteration in range(ITERS):
        weights_bf = weights.astype(jnp.bfloat16)
        partial_pred = (
            jnp.dot(features, weights_bf, preferred_element_type=jnp.float32) * feature_scale
        )
        prediction = lax.psum(partial_pred, ("user", "party"))
        error_rows = (prediction - targets).astype(jnp.bfloat16)
        grad = (
            lax.dot_general(
                features, error_rows, (((0,), (0,)), ((), ())), preferred_element_type=jnp.float32
            )
            * feature_scale
            + ridge_decay * weights
        )
        total_sq = lax.psum(jnp.sum(grad * grad), ("user", "party"))
        mean_sq = total_sq / float(total_features * grad.shape[1])
        weights = weights - ridge_step * grad * lax.rsqrt(mean_sq + 1e-06)
    return (new_factors, weights)


def solution(mesh):
    in_specs = (
        P("party", "user"),
        P("party", "user"),
        P("user", None),
        P(),
        P(),
        P(None, ("user", "party")),
        P(("user", "party"), None),
    )
    out_specs = (P("party", None), P(("user", "party"), None))
    return jax.shard_map(local, mesh=mesh, in_specs=in_specs, out_specs=out_specs, check_vma=False)
```

profile of v0, /device:TPU:0, one launch (start us, length us, event | category | flops | bytes accessed | tf_op | source)
XLA Modules:
  0.0 466.9 jit_solution(16885731106189834640)
XLA Ops:
  8.0 0.0 copy-start
  8.0 0.0 reduce-scatter.2.cloned.1.call-start
  8.1 0.8 compare_and_fusion
  8.9 1.6 gather_fusion
  10.5 0.1 broadcast_select_fusion
  10.6 0.0 copy-done
  10.6 2.1 fusion.14
  12.7 0.0 reduce-scatter.2.cloned.1.call-update
  12.8 0.0 copy-start.2
  12.8 0.0 all-reduce.3.cloned.1.call-start
  12.8 13.4 %convolution_multiply_fusion.2 = f32[512,256]{1,0:T(8,128)} fusion(bf16[512,16384]{1,0:T(8,128)(2,1)} %param.12, bf16[16384,256]{1,0:T(8,128)(2,1)} %param.13), kind=kOutput, calls=%fused_computation.17 | convolution fusion | flops 4295098368 | bytes 25690112 | tf_op jit(solution)/shard_map/dot_general | solution.py:43
  26.3 0.0 all-reduce.3.cloned.1.call-update
  26.3 0.0 all-reduce.5.cloned.1.call-start
  26.3 0.0 copy-done.2
  26.4 12.0 %copy.9 = bf16[16384,256]{0,1:T(8,128)(2,1)} copy(bf16[16384,256]{1,0:T(8,128)(2,1)} %param.13) | data formatting | bytes 16777216 | tf_op args[6]
  38.3 0.7 convert_subtract_fusion.2
  39.1 6.2 %all_gather.6 = f32[64,256]{1,0:T(8,128)S(1)} all-gather(f32[16,256]{1,0:T(8,128)S(1)} %convert_subtract_fusion.2), channel_id=1, replica_groups=mesh['user'=4,'party'=8] {'user'}, dimensions={0}, use_global_device_ids=true | all-gather | bytes 81920 | tf_op jit(solution)/shard_map/all_gather | solution.py:33
  45.3 32.5 %all_gather.7 = f32[512,256]{1,0:T(8,128)S(1)} all-gather(f32[64,256]{1,0:T(8,128)S(1)} %all_gather.6), channel_id=1, replica_groups=mesh['user'=4,'party'=8] {'party'}, dimensions={0}, use_global_device_ids=true | all-gather | bytes 589824 | tf_op jit(solution)/shard_map/all_gather | solution.py:34
  77.8 2.4 scatter_custom_fusion
  80.1 76.9 %all-reduce.3.cloned.1.call-done = f32[512,256]{1,0:T(8,128)} async-done(((f32[512,256]{1,0:T(8,128)}), f32[512,256]{1,0:T(8,128)}) %all-reduce.3.cloned.1.call-update) | async-done | bytes 524304 | tf_op jit(solution)/shard_map/psum | solution.py:45
  157.0 16.1 %multiply_reduce_fusion.1 = (f32[]{:T(128)}, f32[16384,256]{0,1:T(8,128)}) fusion(bf16[16384,256]{0,1:T(8,128)(2,1)} %copy.9, bf16[512,16384]{1,0:T(8,128)(2,1)} %param.12, f32[512,256]{1,0:T(8,128)} %all-reduce.3.cloned.1.call-done, f32[512,256]{1,0:T(8,128)S(1)} %scatter_custom_fusion), kind=kOutput, calls=%fused_computation.12 | convolution fusion | flops 4320395264 | bytes 42991620 | tf_op jit(solution)/shard_map/dot_general | solution.py:48
  173.2 39.5 %psum.29 = f32[]{:T(128)} all-reduce(f32[]{:T(128)} %get-tuple-element.6), channel_id=1, replica_groups=mesh['user'=4,'party'=8] {'user','party'}, use_global_device_ids=true, to_apply=%region_4.5 | all-reduce | flops 1 | bytes 8 | tf_op jit(solution)/shard_map/psum | solution.py:54
  213.4 18.3 %fusion.9 = f32[512,256]{1,0:T(8,128)} fusion(bf16[512,16384]{1,0:T(8,128)(2,1)} %param.12, f32[16384,256]{0,1:T(8,128)} %get-tuple-element.7, f32[]{:T(128)S(6)} %mul.76, bf16[16384,256]{0,1:T(8,128)(2,1)} %copy.9), kind=kOutput, calls=%fused_computation.16 | convolution fusion | flops 4311875584 | bytes 42467332 | tf_op jit(solution)/shard_map/dot_general | solution.py:43
  231.7 0.0 all-reduce.5.cloned.1.call-update
  231.7 127.7 %all-reduce.5.cloned.1.call-done = f32[512,256]{1,0:T(8,128)} async-done(((f32[512,256]{1,0:T(8,128)}), f32[512,256]{1,0:T(8,128)}) %all-reduce.5.cloned.1.call-update) | async-done | bytes 524304 | tf_op jit(solution)/shard_map/psum | solution.py:45
  359.4 21.6 %multiply_reduce_fusion = (f32[]{:T(128)}, f32[16384,256]{0,1:T(8,128)}) fusion(f32[16384,256]{0,1:T(8,128)} %get-tuple-element.7, f32[]{:T(128)S(6)} %mul.76, bf16[16384,256]{0,1:T(8,128)(2,1)} %copy.9, bf16[512,16384]{1,0:T(8,128)(2,1)} %param.12, f32[512,256]{1,0:T(8,128)} %all-reduce.5.cloned.1.call-done, f32[512,256]{1,0:T(8,128)S(1)} %scatter_custom_fusion), kind=kOutput, calls=%fused_computation.11 | convolution fusion | flops 4328783872 | bytes 59768840 | tf_op jit(solution)/shard_map/dot_general | solution.py:48
  381.0 39.3 %psum.31 = f32[]{:T(128)} all-reduce(f32[]{:T(128)} %get-tuple-element.8), channel_id=1, replica_groups=mesh['user'=4,'party'=8] {'user','party'}, use_global_device_ids=true, to_apply=%region_7.8 | all-reduce | flops 1 | bytes 8 | tf_op jit(solution)/shard_map/psum | solution.py:54
  421.0 0.0 copy-start.1
  421.0 20.4 %multiply_subtract_fusion = f32[16384,256]{0,1:T(8,128)} fusion(f32[16384,256]{0,1:T(8,128)} %get-tuple-element.9, f32[]{:T(128)S(6)} %mul.85, f32[16384,256]{0,1:T(8,128)} %get-tuple-element.7, f32[]{:T(128)S(6)} %mul.76, bf16[16384,256]{0,1:T(8,128)(2,1)} %copy.9), kind=kLoop, calls=%fused_computation.10 | loop fusion | flops 20971520 | bytes 58720264 | tf_op jit(solution)/shard_map/sub | solution.py:56
  441.4 17.4 %copy.10 = f32[16384,256]{1,0:T(8,128)} copy(f32[16384,256]{0,1:T(8,128)} %multiply_subtract_fusion) | data formatting | bytes 33554432
  458.8 0.6 copy.14
  459.5 0.0 copy-done.1
  (3 shorter events, 0.0 us)
Async XLA Ops:
  8.0 2.6 copy-start
  8.0 30.3 %reduce-scatter.2.cloned.1.call-start = ((), (), s32[]{:S(2)}) async-start(), calls=%async_computation.1 | async-start | bytes 81920 | tf_op jit(solution)/shard_map/reduce_scatter | solution.py:27
  12.8 13.6 %copy-start.2 = (s32[512]{0:T(512)S(1)}, s32[512]{0:T(512)}, u32[]{:S(2)}) copy-start(s32[512]{0:T(512)} %param.11) | copy-start | bytes 6148
  12.8 144.3 %all-reduce.3.cloned.1.call-start = ((), (), s32[]{:S(2)}) async-start(), calls=%async_computation.2 | async-start | bytes 1048576 | tf_op jit(solution)/shard_map/psum | solution.py:45
  26.3 333.1 %all-reduce.5.cloned.1.call-start = ((), (), s32[]{:S(2)}) async-start(), calls=%async_computation.3 | async-start | bytes 1048576 | tf_op jit(solution)/shard_map/psum | solution.py:45
  421.0 38.5 %copy-start.1 = (bf16[1024,256]{1,0:T(8,128)(2,1)S(1)}, bf16[1024,256]{1,0:T(8,128)(2,1)}, u32[]{:S(2)}) copy-start(bf16[1024,256]{1,0:T(8,128)(2,1)} %param.9) | copy-start | bytes 1572868
Sparse Core Ops, SparseCore 0:
  12.9 22.1 reduce-scatter.1
Sparse Core Ops, SparseCore 1:
  26.4 130.6 all-reduce.2
  231.8 127.5 all-reduce.4
where the time goes:
time: 468 us; the launch traced here: 467 us
  waiting for transfers between devices  205 us (44%)
  blocking collectives  118 us (25%)
  matrix products  71.6 us (15%)
  local copies, waits for them, and re-layouts  34.1 us (7%)
  other arithmetic  22 us (5%)
  between operations  16.9 us (4%)
    psum x2, waiting for transfers between devices, local(): prediction = lax.psum(partial_pred, ('user', 'party'))  205 us
    psum x2, blocking collectives, local(): total_sq = lax.psum(jnp.sum(grad * grad), ('user', 'party'))  78.9 us
    dot_general x2, matrix products, local(): lax.dot_general(features, error_rows, (((0,), (0,)), ((), ())), preferred...  37.7 us
    all_gather x1, blocking collectives, local(): all_factors = lax.all_gather(new_factors, 'party', axis=0, tiled=True)  32.5 us
    dot_general x2, matrix products, local(): jnp.dot(features, weights_bf, preferred_element_type=jnp.float32)  31.7 us
    unnamed x9, local copies, waits for them, and re-layouts  30.1 us
    sub x1, other arithmetic, local(): weights = weights - ridge_step * grad * lax.rsqrt(mean_sq + 1e-06)  20.4 us
  transfers between devices with their start and end apart: 3, of which 2 were waited for; matrix products, arithmetic and copies ran while one was open for 6% of the time, Pallas kernels for 0%

commit v1 on v0

v1 whole, which is shorter than its diff:
```python
import functools

import jax
import jax.numpy as jnp
from jax import lax
from jax.experimental import pallas as pl
from jax.experimental.pallas import tpu as pltpu
from jax.sharding import PartitionSpec as P

learn_rate = 0.05
factor_decay = 1.0
ridge_decay = 0.05
ridge_step = 0.05

MESH = pl.DeviceIdType.MESH
TILE = 256


def dot32(a, b, dims):
    return lax.dot_general(a, b, (dims, ((), ())), preferred_element_type=jnp.float32)


def blocks_of(items):
    count = items // TILE
    return [(i, j) for i in range(count) for j in range(i + 1)]


def rows_of(items, devices):
    used = 2 * items + TILE * len(blocks_of(items))
    step = 8 * devices
    return -(-used // step) * step


def moments_kernel(items, used, share_ref, features_ref, weights_ref, out_ref, norm_ref):
    step = pl.program_id(0)
    gram = 2 * items

    @pl.when(step == 0)
    def _():
        out_ref[...] = jnp.zeros_like(out_ref)
        out_ref[items : 2 * items] = share_ref[...]
        norm_ref[...] = jnp.zeros_like(norm_ref)

    w = weights_ref[...]
    out_ref[0:items] += dot32(features_ref[...], w, ((1,), (0,)))
    for at, (i, j) in enumerate(blocks_of(items)):
        low = gram + at * TILE
        out_ref[low : low + TILE] += dot32(
            features_ref[i * TILE : (i + 1) * TILE],
            features_ref[j * TILE : (j + 1) * TILE],
            ((1,), (1,)),
        )
    wide = w.astype(jnp.float32)
    columns = jnp.sum(wide * wide, axis=0, keepdims=True)
    half = TILE // 2
    norm_ref[...] += columns[:, :half] + columns[:, half:]

    @pl.when(step == pl.num_programs(0) - 1)
    def _():
        out_ref[gram : gram + 1, half:] = norm_ref[...]


def moments(share, features, weights, total_rows):
    items, depth = features.shape
    rank = weights.shape[1]
    block = min(2048, depth)
    return pl.pallas_call(
        functools.partial(moments_kernel, items, total_rows),
        grid=(depth // block,),
        out_shape=jax.ShapeDtypeStruct((total_rows, rank), jnp.float32),
        in_specs=[
            pl.BlockSpec((items, rank), lambda i: (0, 0)),
            pl.BlockSpec((items, block), lambda i: (0, i)),
            pl.BlockSpec((block, rank), lambda i: (i, 0)),
        ],
        out_specs=pl.BlockSpec((total_rows, rank), lambda i: (0, 0)),
        scratch_shapes=[pltpu.VMEM((1, TILE // 2), jnp.float32)],
        compiler_params=pltpu.CompilerParams(vmem_limit_bytes=48 * 2**20),
    )(share, features, weights)


def fit_kernel(
    users, parties, scale, count, part_ref, factors_ref, targets_ref, step_ref, keep_ref,
    work, all_ref, got_a, got_b, got_c, send, recv, back_send, back_recv,
):
    items, rank = factors_ref.shape
    total = work.shape[0]
    size_b, size_c = users, parties // 2
    rows_a = total // 2
    rows_b = rows_a // size_b
    rows_c = rows_b // size_c
    u, p = lax.axis_index("user"), lax.axis_index("party")
    core, at_b, at_c = lax.rem(u, 2), lax.div(u, 2) * 2 + lax.rem(p, 2), lax.div(p, 2)

    def in_b(k):
        to = lax.rem(at_b + k, size_b)
        return to, (lax.div(to, 2) * 2 + core, at_c * 2 + lax.rem(to, 2))

    def in_c(k):
        to = lax.rem(at_c + k, size_c)
        return to, (u, to * 2 + lax.rem(p, 2))

    peer_a = (lax.div(u, 2) * 2 + (1 - core), p)
    low_a = core * rows_a
    low_b = low_a + at_b * rows_b
    low_c = low_b + at_c * rows_c

    def span(low, size):
        return pl.ds(pl.multiple_of(low, 8), size)

    barrier = pltpu.get_barrier_semaphore()
    peers = [peer_a] + [in_b(k)[1] for k in range(1, size_b)] + [in_c(k)[1] for k in range(1, size_c)]
    for peer in peers:
        pl.semaphore_signal(barrier, inc=1, device_id=peer, device_id_type=MESH)
    pl.semaphore_wait(barrier, len(peers))

    def copy(src, dst, sems, at, peer):
        made = pltpu.make_async_remote_copy(
            src_ref=src, dst_ref=dst, send_sem=sems[0].at[at], recv_sem=sems[1].at[at],
            device_id=peer, device_id_type=MESH,
        )
        made.start()
        return made

    out_sems, back_sems = (send, recv), (back_send, back_recv)
    first_a, first_b, first_c = 0, 1, size_b

    first = copy(part_ref.at[span((1 - core) * rows_a, rows_a)], got_a, out_sems, first_a, peer_a)
    first.wait()
    work[span(low_a, rows_a)] = part_ref[span(low_a, rows_a)] + got_a[...]
    second = []
    for k in range(1, size_b):
        to, peer = in_b(k)
        second.append(copy(work.at[span(low_a + to * rows_b, rows_b)], got_b.at[k - 1], out_sems, first_b + k - 1, peer))
    for made in second:
        made.wait()
    value = work[span(low_b, rows_b)]
    for k in range(1, size_b):
        value = value + got_b[k - 1]
    work[span(low_b, rows_b)] = value
    third = []
    for k in range(1, size_c):
        to, peer = in_c(k)
        third.append(copy(work.at[span(low_b + to * rows_c, rows_c)], got_c.at[k - 1], out_sems, first_c + k - 1, peer))
    for made in third:
        made.wait()
    value = work[span(low_c, rows_c)]
    for k in range(1, size_c):
        value = value + got_c[k - 1]
    all_ref[span(low_c, rows_c)] = value

    for low, size, group, start in (
        (low_c, rows_c, [in_c(k)[1] for k in range(1, size_c)], first_c),
        (low_b, rows_b, [in_b(k)[1] for k in range(1, size_b)], first_b),
        (low_a, rows_a, [peer_a], first_a),
    ):
        made = [
            copy(all_ref.at[span(low, size)], all_ref.at[span(low, size)], back_sems, start + k, peer)
            for k, peer in enumerate(group)
        ]
        for one in made:
            one.wait()

    half = TILE // 2
    gram = 2 * items
    norm = jnp.sum(all_ref[gram : gram + 1, half:])
    row = lax.broadcasted_iota(jnp.int32, (TILE, TILE), 0)
    column = lax.broadcasted_iota(jnp.int32, (TILE, TILE), 1)
    corner = all_ref[gram : gram + TILE]
    all_ref[gram : gram + TILE] = jnp.where((row == 0) & (column >= half), corner.T, corner)

    def times_gram(x):
        tiles = items // TILE
        sums = [None] * tiles

        def add(i, term):
            sums[i] = term if sums[i] is None else sums[i] + term

        for at, (i, j) in enumerate(blocks_of(items)):
            block = all_ref[gram + at * TILE : gram + (at + 1) * TILE] * (scale * scale)
            high = block.astype(jnp.bfloat16)
            low = (block - high.astype(jnp.float32)).astype(jnp.bfloat16)
            for piece in (high, low):
                add(i, dot32(piece, x[j * TILE : (j + 1) * TILE], ((1,), (0,))))
                if i != j:
                    add(j, dot32(piece, x[i * TILE : (i + 1) * TILE], ((0,), (0,))))
        return jnp.concatenate(sums, axis=0)

    old = factors_ref[...].astype(jnp.float32)
    targets = old - learn_rate * (all_ref[items : 2 * items] + factor_decay * old)
    targets_ref[...] = targets
    prediction = all_ref[0:items] * scale

    def step_of(square):
        return ridge_step * lax.rsqrt(jnp.maximum(square, 0.0) / count + 1e-06)

    def total_of(x):
        return jnp.sum(jnp.sum(x, axis=0, keepdims=True), axis=1, keepdims=True)

    error1 = (prediction - targets).astype(jnp.bfloat16)
    wide1 = error1.astype(jnp.float32)
    spread1 = times_gram(error1)
    square1 = total_of(wide1 * (spread1 + 2.0 * ridge_decay * prediction)) + ridge_decay**2 * norm
    rate1 = step_of(square1)
    keep1 = 1.0 - ridge_decay * rate1
    second_prediction = keep1 * prediction - rate1 * spread1
    error2 = (second_prediction - targets).astype(jnp.bfloat16)
    wide2 = error2.astype(jnp.float32)
    spread2 = times_gram(error2)
    mixed = wide2 - (ridge_decay * rate1) * wide1
    mixed_spread = spread2 - (ridge_decay * rate1) * spread1
    square2 = (
        total_of(mixed * (mixed_spread + (2.0 * ridge_decay * keep1) * prediction))
        + (ridge_decay * keep1) * (ridge_decay * keep1) * norm
    )
    rate2 = step_of(square2)
    keep2 = 1.0 - ridge_decay * rate2
    step_ref[...] = (scale * (keep2 * rate1 * wide1 + rate2 * wide2)).astype(jnp.bfloat16)
    keep_ref[...] = jnp.broadcast_to(keep1 * keep2, keep_ref.shape)


def fit(part, factors, users, parties, scale, count):
    total, rank = part.shape
    items = factors.shape[0]
    size_b, size_c = users, parties // 2
    rows_a = total // 2
    rows_b = rows_a // size_b
    rows_c = rows_b // size_c
    copies = 1 + (size_b - 1) + (size_c - 1)
    vmem = pl.BlockSpec(memory_space=pltpu.VMEM)
    return pl.pallas_call(
        functools.partial(fit_kernel, users, parties, scale, count),
        out_shape=(
            jax.ShapeDtypeStruct((items, rank), jnp.float32),
            jax.ShapeDtypeStruct((items, rank), jnp.bfloat16),
            jax.ShapeDtypeStruct((8, 128), jnp.float32),
        ),
        in_specs=[vmem] * 2,
        out_specs=(vmem,) * 3,
        scratch_shapes=[
            pltpu.VMEM((total, rank), jnp.float32),
            pltpu.VMEM((total, rank), jnp.float32),
            pltpu.VMEM((rows_a, rank), jnp.float32),
            pltpu.VMEM((size_b - 1, rows_b, rank), jnp.float32),
            pltpu.VMEM((max(size_c - 1, 1), rows_c, rank), jnp.float32),
        ]
        + [pltpu.SemaphoreType.DMA((copies,))] * 4,
        compiler_params=pltpu.CompilerParams(
            collective_id=0, has_side_effects=True, vmem_limit_bytes=56 * 2**20
        ),
    )(part, factors)


def local(users, parties, ratings, rating_mask, user_factors, item_factors, item_index, features, ridge_weights):
    local_items = ratings.shape[0]
    items = item_factors.shape[0]
    party_pos = lax.axis_index("party")
    local_index = lax.dynamic_slice_in_dim(item_index, party_pos * local_items, local_items)
    at_item = local_index[:, None] == jnp.arange(items, dtype=jnp.int32)[None, :]
    tile_rows = jnp.dot(at_item.astype(jnp.bfloat16), item_factors)
    scores = dot32(tile_rows, user_factors, ((1,), (1,)))
    misfit = (rating_mask.astype(jnp.float32) * (scores - ratings.astype(jnp.float32))).astype(jnp.bfloat16)
    partial_grad = jnp.dot(misfit, user_factors, preferred_element_type=jnp.float32)
    share = lax.dot_general(
        at_item.astype(jnp.float32), partial_grad, (((0,), (0,)), ((), ())), precision=lax.Precision.HIGHEST
    )
    devices_all = users * parties
    total_features = features.shape[1] * devices_all
    scale = 1.0 / float(total_features) ** 0.5
    part = moments(share, features, ridge_weights, rows_of(items, devices_all))
    count = float(total_features * ridge_weights.shape[1])
    targets, step, keep = fit(part, item_factors, users, parties, scale, count)
    new_factors = jnp.take(targets, local_index, axis=0)
    weights = ridge_weights.astype(jnp.float32) * keep[0, 0] - dot32(features, step, ((0,), (0,)))
    return (new_factors, weights)


def solution(mesh):
    in_specs = (
        P("party", "user"),
        P("party", "user"),
        P("user", None),
        P(),
        P(),
        P(None, ("user", "party")),
        P(("user", "party"), None),
    )
    out_specs = (P("party", None), P(("user", "party"), None))
    body = functools.partial(local, mesh.shape["user"], mesh.shape["party"])
    return jax.shard_map(body, mesh=mesh, in_specs=in_specs, out_specs=out_specs, check_vma=False)
```

time: 468 us -> 120 us (0.26)
  waiting for transfers between devices: 205 us -> 0 us
  blocking collectives: 118 us -> 0 us
  Pallas kernels: 0 us -> 62.2 us
  matrix products: 71.6 us -> 20.9 us
  other arithmetic: 22 us -> 1.54 us
  between operations: 16.9 us -> 0.7 us
    psum x2 -> x0, waiting for transfers between devices: 205 us -> none  [local(): prediction = lax.psum(partial_pred, ('user', 'party'))]
    psum x2 -> x0, blocking collectives: 78.9 us -> none  [local(): total_sq = lax.psum(jnp.sum(grad * grad), ('user', 'party'))]
    pallas_call x0 -> x2, Pallas kernels: none -> 62.2 us  [the longest x1 46.7 us: fit(): pl.pallas_call(functools.partial(fit_kernel, users, parties, scale, count...]
    dot_general x4 -> x3, matrix products: 69.4 us -> 19.4 us  [the longest x1 17.8 us: dot32(): lax.dot_general(a, b, (dims, ((), ())), preferred_element_type=jnp.float32)]
    all_gather x2 -> x0, blocking collectives: 38.7 us -> none  [the longest x1 32.5 us: local(): all_factors = lax.all_gather(new_factors, 'party', axis=0, tiled=True)]
    sub x2 -> x0, other arithmetic: 21.1 us -> none  [the longest x1 20.4 us: local(): weights = weights - ridge_step * grad * lax.rsqrt(mean_sq + 1e-06)]
    unnamed x9 -> x10, local copies, waits for them, and re-layouts: 30.1 us -> 30.6 us
  transfers between devices with their start and end apart: 3 -> 0, of which waited for: 2 -> 0; matrix products, arithmetic and copies ran while one was open for 6% -> 0% of each run, Pallas kernels for 0% -> 0%
where the time goes in v1:
time: 120 us; the launch traced here: 119 us
  Pallas kernels  62.2 us (52%)
  local copies, waits for them, and re-layouts  33.6 us (28%)
  matrix products  20.9 us (17%)
  other arithmetic  1.54 us (1%)
    pallas_call x1, Pallas kernels, fit(): pl.pallas_call(functools.partial(fit_kernel, users, parties, scale, count...  46.7 us
    unnamed x10, local copies, waits for them, and re-layouts  30.6 us
    dot_general x1, matrix products, dot32(): lax.dot_general(a, b, (dims, ((), ())), preferred_element_type=jnp.float32)  17.8 us
    pallas_call x1, Pallas kernels, moments(): pl.pallas_call(functools.partial(moments_kernel, items, total_rows), grid...  15.4 us

profile of v1, /device:TPU:0, one launch (start us, length us, event | category | flops | bytes accessed | tf_op | source)
XLA Modules:
  0.0 118.9 jit_solution(4625614994722741942)
XLA Ops:
  0.6 0.0 copy-start
  0.7 0.8 compare_and_fusion
  1.5 1.2 fusion.7
  2.6 0.0 copy-done
  2.7 1.5 %fusion.3 = f32[64,256]{1,0:T(8,128)S(1)} fusion(bf16[1024,256]{1,0:T(8,128)(2,1)S(1)} %copy-done, bf16[64,256]{1,0:T(8,128)(2,1)S(1)} %fusion.7, bf16[64,1024]{1,0:T(8,128)(2,1)} %param.7, s32[64,1024]{1,0:T(8,128)} %param.8), kind=kOutput, calls=%fused_computation.6 | convolution fusion | flops 67436544 | bytes 1015808 | tf_op jit(solution)/shard_map/dot_general | solution.py:263
  4.1 0.5 fusion.6.share_ref
  4.6 15.4 %shard_map.86.part_ref = f32[1792,256]{1,0:T(8,128)S(1)} custom-call(f32[512,256]{1,0:T(8,128)S(1)} %fusion.6.share_ref, bf16[512,16384]{1,0:T(8,128)(2,1)} %features_ref.1, bf16[16384,256]{1,0:T(8,128)(2,1)} %weights_ref.1), custom_call_target="tpu_custom_call" | custom-call | tf_op jit(solution)/shard_map/pallas_call | solution.py:67
  20.1 0.0 copy-start.2
  20.1 1.2 %copy-done.2 = f32[1792,256]{1,0:T(8,128)} copy-done((f32[1792,256]{1,0:T(8,128)}, f32[1792,256]{1,0:T(8,128)S(1)}, u32[]{:S(2)}) %copy-start.2) | copy-done | bytes 1835032
  21.3 46.7 %shard_map.87 = (f32[512,256]{1,0:T(8,128)}, bf16[512,256]{1,0:T(8,128)(2,1)}, f32[8,128]{1,0:T(8,128)}) custom-call(f32[1792,256]{1,0:T(8,128)} %copy-done.2, bf16[512,256]{1,0:T(8,128)(2,1)} %factors_ref.1), custom_call_target="tpu_custom_call" | custom-call | tf_op jit(solution)/shard_map/pallas_call | solution.py:231
  68.0 0.0 copy-start.3
  68.1 1.3 %slice.3 = f32[1,1]{1,0:T(1,128)} slice(f32[8,128]{1,0:T(8,128)} %get-tuple-element.6), slice={[0:1], [0:1]} | slice | bytes 8 | tf_op jit(solution)/shard_map/slice | solution.py:274
  69.4 1.7 %gather_fusion = f32[64,256]{1,0:T(8,128)S(1)} fusion(f32[512,256]{1,0:T(8,128)} %get-tuple-element.5, s32[1024]{0:T(1024)S(1)} %pad_clamp_fusion), kind=kCustom, calls=%fused_computation | custom fusion | bytes 131328 | tf_op jit(solution)/shard_map/jit(_take)/gather | solution.py:273
  71.1 0.7 broadcast_select_fusion
  71.8 11.9 %copy.9 = bf16[16384,256]{0,1:T(8,128)(2,1)} copy(bf16[16384,256]{1,0:T(8,128)(2,1)} %weights_ref.1) | data formatting | bytes 16777216 | tf_op args[6]
  83.7 0.0 copy-done.3
  83.7 0.0 copy-start.1
  83.7 17.8 %fusion = f32[16384,256]{0,1:T(8,128)} fusion(bf16[512,256]{1,0:T(8,128)(2,1)S(1)} %copy-done.3, bf16[512,16384]{1,0:T(8,128)(2,1)} %features_ref.1, bf16[16384,256]{0,1:T(8,128)(2,1)} %copy.9, f32[]{:T(128)} %bitcast), kind=kOutput, calls=%fused_computation.2 | convolution fusion | flops 4307550208 | bytes 42205188 | tf_op jit(solution)/shard_map/dot_general | solution.py:20
  101.4 17.4 %copy.10 = f32[16384,256]{1,0:T(8,128)} copy(f32[16384,256]{0,1:T(8,128)} %fusion) | data formatting | bytes 33554432
  118.9 0.0 copy-done.1
  (2 shorter events, 0.0 us)
Async XLA Ops:
  0.6 2.0 %copy-start = (bf16[1024,256]{1,0:T(8,128)(2,1)S(1)}, bf16[1024,256]{1,0:T(8,128)(2,1)}, u32[]{:S(2)}) copy-start(bf16[1024,256]{1,0:T(8,128)(2,1)} %param.9) | copy-start | bytes 1572868
  20.1 1.2 %copy-start.2 = (f32[1792,256]{1,0:T(8,128)}, f32[1792,256]{1,0:T(8,128)S(1)}, u32[]{:S(2)}) copy-start(f32[1792,256]{1,0:T(8,128)S(1)} %shard_map.86.part_ref) | copy-start | bytes 5505028
  68.0 15.6 %copy-start.3 = (bf16[512,256]{1,0:T(8,128)(2,1)S(1)}, bf16[512,256]{1,0:T(8,128)(2,1)}, u32[]{:S(2)}) copy-start(bf16[512,256]{1,0:T(8,128)(2,1)} %get-tuple-element.7) | copy-start | bytes 786436
  83.7 35.2 %copy-start.1 = (bf16[1024,256]{1,0:T(8,128)(2,1)S(1)}, bf16[1024,256]{1,0:T(8,128)(2,1)}, u32[]{:S(2)}) copy-start(bf16[1024,256]{1,0:T(8,128)(2,1)} %param.9) | copy-start | bytes 1572868

commit v2 on v1

--- a/solution.py
+++ b/solution.py
@@ -29,6 +29,13 @@
     used = 2 * items + TILE * len(blocks_of(items))
     step = 8 * devices
     return -(-used // step) * step
+
+
+def chunks_of(total, devices):
+    unit = 8 * devices
+    units = total // unit
+    count = min(3, units)
+    return [unit * (units // count + (1 if i < units % count else 0)) for i in range(count)]
 
 
 def moments_kernel(items, used, share_ref, features_ref, weights_ref, out_ref, norm_ref):
@@ -86,9 +93,6 @@
     items, rank = factors_ref.shape
     total = work.shape[0]
     size_b, size_c = users, parties // 2
-    rows_a = total // 2
-    rows_b = rows_a // size_b
-    rows_c = rows_b // size_c
     u, p = lax.axis_index("user"), lax.axis_index("party")
     core, at_b, at_c = lax.rem(u, 2), lax.div(u, 2) * 2 + lax.rem(p, 2), lax.div(p, 2)
 
@@ -101,9 +105,6 @@
         return to, (u, to * 2 + lax.rem(p, 2))
 
     peer_a = (lax.div(u, 2) * 2 + (1 - core), p)
-    low_a = core * rows_a
-    low_b = low_a + at_b * rows_b
-    low_c = low_b + at_c * rows_c
 
     def span(low, size):
         return pl.ds(pl.multiple_of(low, 8), size)
@@ -125,39 +126,74 @@
     out_sems, back_sems = (send, recv), (back_send, back_recv)
     first_a, first_b, first_c = 0, 1, size_b
 
-    first = copy(part_ref.at[span((1 - core) * rows_a, rows_a)], got_a, out_sems, first_a, peer_a)
-    first.wait()
-    work[span(low_a, rows_a)] = part_ref[span(low_a, rows_a)] + got_a[...]
-    second = []
-    for k in range(1, size_b):
-        to, peer = in_b(k)
-        second.append(copy(work.at[span(low_a + to * rows_b, rows_b)], got_b.at[k - 1], out_sems, first_b + k - 1, peer))
-    for made in second:
-        made.wait()
-    value = work[span(low_b, rows_b)]
-    for k in range(1, size_b):
-        value = value + got_b[k - 1]
-    work[span(low_b, rows_b)] = value
-    third = []
-    for k in range(1, size_c):
-        to, peer = in_c(k)
-        third.append(copy(work.at[span(low_b + to * rows_c, rows_c)], got_c.at[k - 1], out_sems, first_c + k - 1, peer))
-    for made in third:
-        made.wait()
-    value = work[span(low_c, rows_c)]
-    for k in range(1, size_c):
-        value = value + got_c[k - 1]
-    all_ref[span(low_c, rows_c)] = value
-
-    for low, size, group, start in (
-        (low_c, rows_c, [in_c(k)[1] for k in range(1, size_c)], first_c),
-        (low_b, rows_b, [in_b(k)[1] for k in range(1, size_b)], first_b),
-        (low_a, rows_a, [peer_a], first_a),
-    ):
-        made = [
+    per_chunk = 1 + (size_b - 1) + (size_c - 1)
+    chunks = []
+    base = 0
+    for at, rows in enumerate(chunks_of(total, users * parties)):
+        a, b, c = rows // 2, rows // 2 // size_b, rows // 2 // size_b // size_c
+        chunks.append((base, a, b, c, base // 2, base // 2 // size_b, base // 2 // size_b // size_c, at * per_chunk))
+        base += rows
+
+    def lows(base, a, b, c):
+        low_a = base + core * a
+        low_b = low_a + at_b * b
+        return low_a, low_b, low_b + at_c * c
+
+    first, second, third = [], [], []
+    for base, a, b, c, in_a, _, _, sem in chunks:
+        first.append(copy(part_ref.at[span(base + (1 - core) * a, a)], got_a.at[pl.ds(in_a, a)], out_sems, sem + first_a, peer_a))
+    for at, (base, a, b, c, in_a, slot_b, _, sem) in enumerate(chunks):
+        low_a, low_b, low_c = lows(base, a, b, c)
+        first[at].wait()
+        work[span(low_a, a)] = part_ref[span(low_a, a)] + got_a[in_a : in_a + a]
+        made = []
+        for k in range(1, size_b):
+            to, peer = in_b(k)
+            made.append(copy(work.at[span(low_a + to * b, b)], got_b.at[k - 1, pl.ds(slot_b, b)], out_sems, sem + first_b + k - 1, peer))
+        second.append(made)
+    for at, (base, a, b, c, _, slot_b, slot_c, sem) in enumerate(chunks):
+        low_a, low_b, low_c = lows(base, a, b, c)
+        for one in second[at]:
+            one.wait()
+        value = work[span(low_b, b)]
+        for k in range(1, size_b):
+            value = value + got_b[k - 1, slot_b : slot_b + b]
+        work[span(low_b, b)] = value
+        made = []
+        for k in range(1, size_c):
+            to, peer = in_c(k)
+            made.append(copy(work.at[span(low_b + to * c, c)], got_c.at[k - 1, pl.ds(slot_c, c)], out_sems, sem + first_c + k - 1, peer))
+        third.append(made)
+
+    def back(low, size, group, start):
+        return [
             copy(all_ref.at[span(low, size)], all_ref.at[span(low, size)], back_sems, start + k, peer)
             for k, peer in enumerate(group)
         ]
+
+    peers_b = [in_b(k)[1] for k in range(1, size_b)]
+    peers_c = [in_c(k)[1] for k in range(1, size_c)]
+    stage_c, stage_b, stage_a = [], [], []
+    for at, (base, a, b, c, _, _, slot_c, sem) in enumerate(chunks):
+        low_a, low_b, low_c = lows(base, a, b, c)
+        for one in third[at]:
+            one.wait()
+        value = work[span(low_c, c)]
+        for k in range(1, size_c):
+            value = value + got_c[k - 1, slot_c : slot_c + c]
+        all_ref[span(low_c, c)] = value
+        stage_c.append(back(low_c, c, peers_c, sem + first_c))
+    for at, (base, a, b, c, _, _, _, sem) in enumerate(chunks):
+        low_a, low_b, low_c = lows(base, a, b, c)
+        for one in stage_c[at]:
+            one.wait()
+        stage_b.append(back(low_b, b, peers_b, sem + first_b))
+    for at, (base, a, b, c, _, _, _, sem) in enumerate(chunks):
+        low_a, low_b, low_c = lows(base, a, b, c)
+        for one in stage_b[at]:
+            one.wait()
+        stage_a.append(back(low_a, a, [peer_a], sem + first_a))
+    for made in stage_a:
         for one in made:
             one.wait()
 
@@ -226,7 +262,7 @@
     rows_a = total // 2
     rows_b = rows_a // size_b
     rows_c = rows_b // size_c
-    copies = 1 + (size_b - 1) + (size_c - 1)
+    copies = (1 + (size_b - 1) + (size_c - 1)) * len(chunks_of(total, users * parties))
     vmem = pl.BlockSpec(memory_space=pltpu.VMEM)
     return pl.pallas_call(
         functools.partial(fit_kernel, users, parties, scale, count),
@@ -251,6 +287,30 @@
     )(part, factors)
 
 
+def last_kernel(features_ref, weights_ref, step_ref, keep_ref, out_ref):
+    change = dot32(features_ref[...], step_ref[...], ((0,), (0,)))
+    out_ref[...] = weights_ref[...].astype(jnp.float32) * keep_ref[0:1, 0:1] - change
+
+
+def last(features, weights, step, keep):
+    items, depth = features.shape
+    rank = weights.shape[1]
+    block = min(1024, depth)
+    return pl.pallas_call(
+        last_kernel,
+        grid=(depth // block,),
+        out_shape=jax.ShapeDtypeStruct((depth, rank), jnp.float32),
+        in_specs=[
+            pl.BlockSpec((items, block), lambda i: (0, i)),
+            pl.BlockSpec((block, rank), lambda i: (i, 0)),
+            pl.BlockSpec((items, rank), lambda i: (0, 0)),
+            pl.BlockSpec(keep.shape, lambda i: (0, 0)),
+        ],
+        out_specs=pl.BlockSpec((block, rank), lambda i: (i, 0)),
+        compiler_params=pltpu.CompilerParams(vmem_limit_bytes=48 * 2**20),
+    )(features, weights, step, keep)
+
+
 def local(users, parties, ratings, rating_mask, user_factors, item_factors, item_index, features, ridge_weights):
     local_items = ratings.shape[0]
     items = item_factors.shape[0]
@@ -271,7 +331,7 @@
     count = float(total_features * ridge_weights.shape[1])
     targets, step, keep = fit(part, item_factors, users, parties, scale, count)
     new_factors = jnp.take(targets, local_index, axis=0)
-    weights = ridge_weights.astype(jnp.float32) * keep[0, 0] - dot32(features, step, ((0,), (0,)))
+    weights = last(features, ridge_weights, step, keep)
     return (new_factors, weights)
 
 

time: 120 us -> 88.2 us (0.73)
  local copies, waits for them, and re-layouts: 33.6 us -> 4.56 us
  matrix products: 20.9 us -> 3.13 us
  Pallas kernels: 62.2 us -> 77.7 us
    unnamed x10 -> x8, local copies, waits for them, and re-layouts: 30.6 us -> 2.86 us
    pallas_call x0 -> x1, Pallas kernels: none -> 22 us  [last(): pl.pallas_call(last_kernel, grid=(depth // block,), out_shape=jax.ShapeDt...]
    dot_general x1 -> x0, matrix products: 17.8 us -> none  [dot32(): lax.dot_general(a, b, (dims, ((), ())), preferred_element_type=jnp.float32)]
    pallas_call x1, Pallas kernels: 46.7 us -> 40.3 us  [fit(): pl.pallas_call(functools.partial(fit_kernel, users, parties, scale, count...]
    slice x1 -> x0, local copies, waits for them, and re-layouts: 1.31 us -> none  [local(): keep[0, 0]]
where the time goes in v2:
time: 88.2 us; the launch traced here: 87.6 us
  Pallas kernels  77.7 us (88%)
  local copies, waits for them, and re-layouts  4.56 us (5%)
  matrix products  3.13 us (4%)
  other arithmetic  1.54 us (2%)
    pallas_call x1, Pallas kernels, fit(): pl.pallas_call(functools.partial(fit_kernel, users, parties, scale, count...  40.3 us
    pallas_call x1, Pallas kernels, last(): pl.pallas_call(last_kernel, grid=(depth // block,), out_shape=jax.ShapeDt...  22 us
    pallas_call x1, Pallas kernels, moments(): pl.pallas_call(functools.partial(moments_kernel, items, total_rows), grid...  15.4 us
    unnamed x8, local copies, waits for them, and re-layouts  2.86 us

profile of v2, /device:TPU:0, one launch (start us, length us, event | category | flops | bytes accessed | tf_op | source)
XLA Modules:
  0.0 87.6 jit_solution(2714878414107541911)
XLA Ops:
  0.6 0.0 copy-start
  0.6 0.8 compare_and_fusion
  1.5 1.2 %fusion.6 = bf16[64,256]{1,0:T(8,128)(2,1)S(1)} fusion(bf16[512,256]{1,0:T(8,128)(2,1)} %factors_ref.1, s32[64]{0:T(128)S(1)} %get-tuple-element.9), kind=kOutput, calls=%fused_computation.9 | convolution fusion | flops 16809984 | bytes 295168 | tf_op jit(solution)/shard_map/dot_general | solution.py:320
  2.6 0.0 copy-done
  2.6 1.5 %fusion.2 = f32[64,256]{1,0:T(8,128)S(1)} fusion(bf16[1024,256]{1,0:T(8,128)(2,1)S(1)} %copy-done, bf16[64,256]{1,0:T(8,128)(2,1)S(1)} %fusion.6, bf16[64,1024]{1,0:T(8,128)(2,1)} %param.7, s32[64,1024]{1,0:T(8,128)} %param.8), kind=kOutput, calls=%fused_computation.4 | convolution fusion | flops 67436544 | bytes 1015808 | tf_op jit(solution)/shard_map/dot_general | solution.py:323
  4.1 0.5 fusion.5.share_ref
  4.6 15.4 %shard_map.86.part_ref = f32[1792,256]{1,0:T(8,128)S(1)} custom-call(f32[512,256]{1,0:T(8,128)S(1)} %fusion.5.share_ref, bf16[512,16384]{1,0:T(8,128)(2,1)} %features_ref.3, bf16[16384,256]{1,0:T(8,128)(2,1)} %weights_ref.3), custom_call_target="tpu_custom_call" | custom-call | tf_op jit(solution)/shard_map/pallas_call | solution.py:74
  20.1 0.0 copy-start.1
  20.1 1.2 %copy-done.1 = f32[1792,256]{1,0:T(8,128)} copy-done((f32[1792,256]{1,0:T(8,128)}, f32[1792,256]{1,0:T(8,128)S(1)}, u32[]{:S(2)}) %copy-start.1) | copy-done | bytes 1835032
  21.3 40.3 %shard_map.87 = (f32[512,256]{1,0:T(8,128)}, bf16[512,256]{1,0:T(8,128)(2,1)}, f32[8,128]{1,0:T(8,128)}) custom-call(f32[1792,256]{1,0:T(8,128)} %copy-done.1, bf16[512,256]{1,0:T(8,128)(2,1)} %factors_ref.1), custom_call_target="tpu_custom_call" | custom-call | tf_op jit(solution)/shard_map/pallas_call | solution.py:267
  61.6 1.7 %gather_fusion = f32[64,256]{1,0:T(8,128)S(1)} fusion(f32[512,256]{1,0:T(8,128)} %get-tuple-element.5, s32[1024]{0:T(1024)S(1)} %pad_clamp_fusion), kind=kCustom, calls=%fused_computation | custom fusion | bytes 131328 | tf_op jit(solution)/shard_map/jit(_take)/gather | solution.py:333
  63.3 0.7 broadcast_select_fusion
  64.0 0.0 copy-start.2
  64.0 0.9 %copy-done.2 = bf16[512,256]{1,0:T(8,128)(2,1)S(1)} copy-done((bf16[512,256]{1,0:T(8,128)(2,1)S(1)}, bf16[512,256]{1,0:T(8,128)(2,1)}, u32[]{:S(2)}) %copy-start.2) | copy-done | bytes 262168
  64.9 0.0 copy-start.3
  64.9 0.7 copy-done.3
  65.6 22.0 %shard_map.88 = f32[16384,256]{1,0:T(8,128)} custom-call(bf16[512,16384]{1,0:T(8,128)(2,1)} %features_ref.3, bf16[16384,256]{1,0:T(8,128)(2,1)} %weights_ref.3, bf16[512,256]{1,0:T(8,128)(2,1)S(1)} %copy-done.2, f32[8,128]{1,0:T(8,128)S(1)} %copy-done.3), custom_call_target="tpu_custom_call" | custom-call | tf_op jit(solution)/shard_map/pallas_call | solution.py:299
  (2 shorter events, 0.0 us)
Async XLA Ops:
  0.6 2.0 %copy-start = (bf16[1024,256]{1,0:T(8,128)(2,1)S(1)}, bf16[1024,256]{1,0:T(8,128)(2,1)}, u32[]{:S(2)}) copy-start(bf16[1024,256]{1,0:T(8,128)(2,1)} %param.9) | copy-start | bytes 1572868
  20.1 1.2 %copy-start.1 = (f32[1792,256]{1,0:T(8,128)}, f32[1792,256]{1,0:T(8,128)S(1)}, u32[]{:S(2)}) copy-start(f32[1792,256]{1,0:T(8,128)S(1)} %shard_map.86.part_ref) | copy-start | bytes 5505028
  64.0 0.9 %copy-start.2 = (bf16[512,256]{1,0:T(8,128)(2,1)S(1)}, bf16[512,256]{1,0:T(8,128)(2,1)}, u32[]{:S(2)}) copy-start(bf16[512,256]{1,0:T(8,128)(2,1)} %get-tuple-element.6.step_ref) | copy-start | bytes 786436
  64.9 0.7 copy-start.3

commit v3 on v2

--- a/solution.py
+++ b/solution.py
@@ -70,7 +70,7 @@
 def moments(share, features, weights, total_rows):
     items, depth = features.shape
     rank = weights.shape[1]
-    block = min(2048, depth)
+    block = min(4096, depth)
     return pl.pallas_call(
         functools.partial(moments_kernel, items, total_rows),
         grid=(depth // block,),
@@ -295,7 +295,7 @@
 def last(features, weights, step, keep):
     items, depth = features.shape
     rank = weights.shape[1]
-    block = min(1024, depth)
+    block = min(4096, depth)
     return pl.pallas_call(
         last_kernel,
         grid=(depth // block,),

time: 88.2 us -> 80.3 us (0.910)
  Pallas kernels: 77.7 us -> 70.1 us
    pallas_call x1, Pallas kernels: 22 us -> 15.2 us  [last(): pl.pallas_call(last_kernel, grid=(depth // block,), out_shape=jax.ShapeDt...]
where the time goes in v3:
time: 80.3 us; the launch traced here: 80 us
  Pallas kernels  70.1 us (87%)
  local copies, waits for them, and re-layouts  4.56 us (6%)
  matrix products  3.13 us (4%)
  other arithmetic  1.54 us (2%)
    pallas_call x1, Pallas kernels, fit(): pl.pallas_call(functools.partial(fit_kernel, users, parties, scale, count...  40.3 us
    pallas_call x1, Pallas kernels, last(): pl.pallas_call(last_kernel, grid=(depth // block,), out_shape=jax.ShapeDt...  15.2 us
    pallas_call x1, Pallas kernels, moments(): pl.pallas_call(functools.partial(moments_kernel, items, total_rows), grid...  14.6 us
    unnamed x8, local copies, waits for them, and re-layouts  2.86 us
    gather x1, local copies, waits for them, and re-layouts, local(): new_factors = jnp.take(targets, local_index, axis=0)  1.69 us

profile of v3, /device:TPU:0, one launch (start us, length us, event | category | flops | bytes accessed | tf_op | source)
XLA Modules:
  0.0 80.0 jit_solution(14195904786255228621)
XLA Ops:
  0.6 0.0 copy-start
  0.6 0.8 %compare_and_fusion = (pred[64]{0:T(512)(128)(4,1)S(1)}, s32[64]{0:T(128)S(1)}) fusion(s32[512]{0:T(512)} %param.11, s32[]{:T(128)S(6)} %select_n.12), kind=kLoop, calls=%fused_computation.15 | loop fusion | flops 384 | bytes 580 | tf_op jit(solution)/shard_map/jit(_take)/and | solution.py:333
  1.5 1.2 %fusion.6 = bf16[64,256]{1,0:T(8,128)(2,1)S(1)} fusion(bf16[512,256]{1,0:T(8,128)(2,1)} %factors_ref.1, s32[64]{0:T(128)S(1)} %get-tuple-element.9), kind=kOutput, calls=%fused_computation.9 | convolution fusion | flops 16809984 | bytes 295168 | tf_op jit(solution)/shard_map/dot_general | solution.py:320
  2.6 0.0 copy-done
  2.6 1.5 %fusion.2 = f32[64,256]{1,0:T(8,128)S(1)} fusion(bf16[1024,256]{1,0:T(8,128)(2,1)S(1)} %copy-done, bf16[64,256]{1,0:T(8,128)(2,1)S(1)} %fusion.6, bf16[64,1024]{1,0:T(8,128)(2,1)} %param.7, s32[64,1024]{1,0:T(8,128)} %param.8), kind=kOutput, calls=%fused_computation.4 | convolution fusion | flops 67436544 | bytes 1015808 | tf_op jit(solution)/shard_map/dot_general | solution.py:323
  4.1 0.5 fusion.5.share_ref
  4.6 14.6 %shard_map.86.part_ref = f32[1792,256]{1,0:T(8,128)S(1)} custom-call(f32[512,256]{1,0:T(8,128)S(1)} %fusion.5.share_ref, bf16[512,16384]{1,0:T(8,128)(2,1)} %features_ref.3, bf16[16384,256]{1,0:T(8,128)(2,1)} %weights_ref.3), custom_call_target="tpu_custom_call" | custom-call | tf_op jit(solution)/shard_map/pallas_call | solution.py:74
  19.2 0.0 copy-start.1
  19.2 1.2 %copy-done.1 = f32[1792,256]{1,0:T(8,128)} copy-done((f32[1792,256]{1,0:T(8,128)}, f32[1792,256]{1,0:T(8,128)S(1)}, u32[]{:S(2)}) %copy-start.1) | copy-done | bytes 1835032
  20.4 40.3 %shard_map.87 = (f32[512,256]{1,0:T(8,128)}, bf16[512,256]{1,0:T(8,128)(2,1)}, f32[8,128]{1,0:T(8,128)}) custom-call(f32[1792,256]{1,0:T(8,128)} %copy-done.1, bf16[512,256]{1,0:T(8,128)(2,1)} %factors_ref.1), custom_call_target="tpu_custom_call" | custom-call | tf_op jit(solution)/shard_map/pallas_call | solution.py:267
  60.7 1.7 %gather_fusion = f32[64,256]{1,0:T(8,128)S(1)} fusion(f32[512,256]{1,0:T(8,128)} %get-tuple-element.5, s32[1024]{0:T(1024)S(1)} %pad_clamp_fusion), kind=kCustom, calls=%fused_computation | custom fusion | bytes 131328 | tf_op jit(solution)/shard_map/jit(_take)/gather | solution.py:333
  62.4 0.7 broadcast_select_fusion
  63.1 0.0 copy-start.2
  63.1 0.9 %copy-done.2 = bf16[512,256]{1,0:T(8,128)(2,1)S(1)} copy-done((bf16[512,256]{1,0:T(8,128)(2,1)S(1)}, bf16[512,256]{1,0:T(8,128)(2,1)}, u32[]{:S(2)}) %copy-start.2) | copy-done | bytes 262168
  64.1 0.0 copy-start.3
  64.1 0.7 copy-done.3
  64.8 15.2 %shard_map.88 = f32[16384,256]{1,0:T(8,128)} custom-call(bf16[512,16384]{1,0:T(8,128)(2,1)} %features_ref.3, bf16[16384,256]{1,0:T(8,128)(2,1)} %weights_ref.3, bf16[512,256]{1,0:T(8,128)(2,1)S(1)} %copy-done.2, f32[8,128]{1,0:T(8,128)S(1)} %copy-done.3), custom_call_target="tpu_custom_call" | custom-call | tf_op jit(solution)/shard_map/pallas_call | solution.py:299
  (2 shorter events, 0.0 us)
Async XLA Ops:
  0.6 2.0 %copy-start = (bf16[1024,256]{1,0:T(8,128)(2,1)S(1)}, bf16[1024,256]{1,0:T(8,128)(2,1)}, u32[]{:S(2)}) copy-start(bf16[1024,256]{1,0:T(8,128)(2,1)} %param.9) | copy-start | bytes 1572868
  19.2 1.2 %copy-start.1 = (f32[1792,256]{1,0:T(8,128)}, f32[1792,256]{1,0:T(8,128)S(1)}, u32[]{:S(2)}) copy-start(f32[1792,256]{1,0:T(8,128)S(1)} %shard_map.86.part_ref) | copy-start | bytes 5505028
  63.1 0.9 %copy-start.2 = (bf16[512,256]{1,0:T(8,128)(2,1)S(1)}, bf16[512,256]{1,0:T(8,128)(2,1)}, u32[]{:S(2)}) copy-start(bf16[512,256]{1,0:T(8,128)(2,1)} %get-tuple-element.6.step_ref) | copy-start | bytes 786436
  64.1 0.7 copy-start.3
